TPU v7x, 32 devices: a whole 2x2x4 slice. The times are simulated.
32 devices in a mesh: parts: 2 (over x), slab: 16 (over z, y, core).
Axes of the slice: x: 2, y: 2, z: 4, core: 2. Of those that a mesh axis runs over, the one named last changes fastest.
Arguments:
- e_field: float32 [3, 512, 64, 128], P(None, ('parts', 'slab')), parts along dimension 1, may hold values from -6 to 6
- h_field: float32 [3, 512, 64, 128], P(None, ('parts', 'slab')), parts along dimension 1, may hold values from -6 to 6
- phasor_re: float32 [3, 512, 64, 128], P(None, ('parts', 'slab')), parts along dimension 1, may hold values from -12 to 12
- phasor_im: float32 [3, 512, 64, 128], P(None, ('parts', 'slab')), parts along dimension 1, may hold values from -12 to 12
- tissue: int32 [512, 64, 128], P(('parts', 'slab')), parts along dimension 0, may hold values from 0 to 77, as said below
- sigma_table: float32 [77], replicated, may hold values from 0.004 to 0.25
- eps_table: float32 [77], replicated, may hold values from 5 to 80
- density_table: float32 [77], replicated, may hold values from 0.9 to 1.9
- brick_anchor: int32 [3, 5120], P(None, ('parts', 'slab')), parts along dimension 1, may hold values from 0 to 120, as said below
- brick_helper: int32 [5120], P(('parts', 'slab')), parts along dimension 0, may hold values from 0 to 15, as said below
- brick_count: int32 [32], P(('parts', 'slab')), parts along dimension 0, may hold values from 16 to 160, as said below
Outputs:
- e_final: float32 [3, 512, 64, 128], P(None, ('parts', 'slab')), parts along dimension 1
- h_final: float32 [3, 512, 64, 128], P(None, ('parts', 'slab')), parts along dimension 1
- sar_table: float32 [5120, 512], P(('parts', 'slab')), parts along dimension 0
There are 2 independent parts, one for each index of `parts`. A program takes and returns all parts, laid end to end along the dimension named above; an argument that names none is the same for every part. Nothing has to cross between parts.
Inputs may be any that keep to these rules, and one draw needn't show every extreme that they name: 0 marks air; tissue k > 0 takes entry k - 1 of each table. `brick_count`: every device lists 10 + 6 or more bricks; some device lists 160. `brick_helper`: among the 160 entries of one device no helper appears more than 10 times; in every draw some helper receives 10 listed bricks from every device. `brick_anchor`: row 0 lies in 0 to 8, row 1 in 0 to 56, row 2 in 0 to 120: every brick lies inside its owner's block.
All inputs are finite; a program needn't handle non-finite values.
Results may differ from a plain program's by a relative error of at most 0.00016.
Values sent between devices are 32-bit elements; how exact they have to be, the bound alone decides.
A program may use at most 64 MiB of HBM per device.

v0:
```python
import math

import jax
import jax.numpy as jnp
from jax import lax
from jax.sharding import PartitionSpec as P

STEPS = 6
APRON = 10
BRICK = 8
PERIOD = 2600
START = 325


COURANT = 0.5
FLOOR_SHARE = 0.2


def shifted(block, axis, distance):
    devices = range(lax.axis_size(axis))
    route = [(i - distance, i) for i in devices if i - distance in devices]
    return lax.ppermute(block, axis, route)


def with_halo(array, sides, width):
    for axis, dim in sides:
        devices, length = (lax.axis_size(axis), array.shape[dim])
        up = [(i, (i + 1) % devices) for i in range(devices - 1)]
        down = [(j, i) for i, j in up]
        last = lax.slice_in_dim(array, length - width, length, axis=dim)
        leading = lax.slice_in_dim(array, 0, width, axis=dim)
        before = lax.ppermute(last, axis, up)
        after = lax.ppermute(leading, axis, down)
        array = jnp.concatenate([before, array, after], axis=dim)
    return array


def forward_diff(values, axis, tail_face):
    if tail_face is None:
        tail_face = jnp.zeros_like(lax.slice_in_dim(values, 0, 1, axis=axis))
    moved = jnp.concatenate(
        [lax.slice_in_dim(values, 1, values.shape[axis], axis=axis), tail_face], axis
    )
    return moved - values


def backward_diff(values, axis, head_face):
    if head_face is None:
        head_face = jnp.zeros_like(lax.slice_in_dim(values, 0, 1, axis=axis))
    moved = jnp.concatenate(
        [head_face, lax.slice_in_dim(values, 0, values.shape[axis] - 1, axis=axis)], axis
    )
    return values - moved


def magnetic_step(electric, magnetic, ahead_face):
    face_y = ahead_face[0]
    face_z = ahead_face[1]
    mag_x = magnetic[0] - COURANT * (
        forward_diff(electric[2], 1, None) - forward_diff(electric[1], 2, None)
    )
    mag_y = magnetic[1] - COURANT * (
        forward_diff(electric[0], 2, None) - forward_diff(electric[2], 0, face_z)
    )
    mag_z = magnetic[2] - COURANT * (
        forward_diff(electric[1], 0, face_y) - forward_diff(electric[0], 1, None)
    )
    result = jnp.stack([mag_x, mag_y, mag_z])
    return result


def electric_step(electric, magnetic, coef_keep, coef_curl, behind_face):
    face_y = behind_face[0]
    face_z = behind_face[1]
    ele_x = coef_keep * electric[0] + coef_curl * (
        backward_diff(magnetic[2], 1, None) - backward_diff(magnetic[1], 2, None)
    )
    ele_y = coef_keep * electric[1] + coef_curl * (
        backward_diff(magnetic[0], 2, None) - backward_diff(magnetic[2], 0, face_z)
    )
    ele_z = coef_keep * electric[2] + coef_curl * (
        backward_diff(magnetic[1], 0, face_y) - backward_diff(magnetic[0], 1, None)
    )
    result = jnp.stack([ele_x, ele_y, ele_z])
    return result


def materials(tissue, sigma_table, eps_table, density_table):
    labels = jnp.arange(1, sigma_table.shape[0] + 1, dtype=jnp.int32)[:, None]
    table = jnp.stack([sigma_table, eps_table - 1.0, density_table])
    layers = tissue.reshape(tissue.shape[0], -1)

    def one_layer(layer):
        onehot = (layer[None, :] == labels).astype(jnp.float32)
        product = jnp.dot(table, onehot, precision=lax.Precision.HIGHEST)
        return (product[0], product[1], product[2])

    sigma_rows, eps_rows, mass_rows = lax.map(one_layer, layers)
    return (
        sigma_rows.reshape(tissue.shape),
        1.0 + eps_rows.reshape(tissue.shape),
        mass_rows.reshape(tissue.shape),
    )


def band_matrix(count_out, count_in, lowest):
    offset = (
        jnp.arange(count_in, dtype=jnp.int32)[None, :]
        - jnp.arange(count_out, dtype=jnp.int32)[:, None]
    )
    return ((offset >= lowest) & (offset <= lowest + 2 * APRON)).astype(jnp.float32)


def body(
    e_field,
    h_field,
    phasor_re,
    phasor_im,
    tissue,
    sigma_table,
    eps_table,
    density_table,
    brick_anchor,
    brick_helper,
    brick_count,
):
    width = e_field.shape[1]
    across_y = e_field.shape[2]
    across_z = e_field.shape[3]
    conductivity, eps_rel, density = materials(tissue, sigma_table, eps_table, density_table)
    damping = conductivity / (2.0 * eps_rel)
    coef_keep = (1.0 - damping) / (1.0 + damping)
    coef_curl = COURANT / (eps_rel * (1.0 + damping))
    electric, magnetic = (e_field, h_field)
    re_total, im_total = (phasor_re, phasor_im)
    for step in range(STEPS):
        ahead_face = shifted(electric[1:3, 0:1], "slab", -1)
        magnetic = magnetic_step(electric, magnetic, ahead_face)
        behind_face = shifted(magnetic[1:3, width - 1 : width], "slab", 1)
        electric = electric_step(electric, magnetic, coef_keep, coef_curl, behind_face)
        phase_angle = 2.0 * math.pi * (START + step + 1) / PERIOD
        re_total = re_total + math.cos(phase_angle) * electric
        im_total = im_total - math.sin(phase_angle) * electric
    heating = 0.5 * conductivity * jnp.sum(re_total * re_total + im_total * im_total, axis=0)
    sources = jnp.stack([heating, density])
    wide = with_halo(sources, (("slab", 1),), APRON)
    floor_mass = FLOOR_SHARE * (2 * APRON + 1) ** 3
    count_slots = brick_helper.shape[0]
    edge = BRICK
    reach = 2 * APRON + 1
    along_z = jnp.dot(
        wide.reshape(-1, across_z),
        band_matrix(across_z, across_z, -APRON),
        precision=lax.Precision.HIGHEST,
    ).reshape(wide.shape)
    padded_y = jnp.pad(along_z, ((0, 0), (0, 0), (APRON, APRON), (0, 0)))
    along_y = padded_y[:, :, 0:across_y]
    for offset in range(1, reach):
        along_y = along_y + padded_y[:, :, offset : offset + across_y]
    along_x = along_y[:, 0:width]
    for offset in range(1, reach):
        along_x = along_x + along_y[:, offset : offset + width]
    sar_avg = along_x[0] / jnp.maximum(along_x[1], floor_mass)
    steps_in = jnp.arange(edge, dtype=jnp.int32)
    flat_index = (
        (
            (brick_anchor[0][:, None, None, None] + steps_in[None, :, None, None]) * across_y
            + brick_anchor[1][:, None, None, None]
            + steps_in[None, None, :, None]
        )
        * across_z
        + brick_anchor[2][:, None, None, None]
        + steps_in[None, None, None, :]
    )
    brick_cores = jnp.take(sar_avg.reshape(-1), flat_index.reshape(count_slots, edge**3), axis=0)
    slab_count = lax.axis_size("slab")
    capacity = max(2, (count_slots + slab_count - 1) // slab_count)
    slot_index = jnp.arange(count_slots, dtype=jnp.int32)
    live_slots = slot_index < brick_count[0]
    earlier = (brick_helper[:, None] == brick_helper[None, :]) & (
        slot_index[None, :] < slot_index[:, None]
    )
    slot_rank = jnp.sum(earlier.astype(jnp.int32), axis=1)
    target = jnp.where(live_slots, brick_helper * capacity + slot_rank, -1)
    route = (jnp.arange(slab_count * capacity, dtype=jnp.int32)[:, None] == target[None, :]).astype(
        jnp.float32
    )
    outgoing = jnp.dot(route, brick_cores, precision=lax.Precision.HIGHEST).reshape(
        slab_count, capacity, edge**3
    )
    incoming = lax.all_to_all(outgoing, "slab", split_axis=0, concat_axis=0, tiled=True)
    sar_table = incoming.reshape(slab_count * capacity, edge**3)
    return (electric, magnetic, sar_table)


def solution(mesh):
    return jax.shard_map(
        body,
        mesh=mesh,
        in_specs=(
            P(None, ("parts", "slab"), None, None),
            P(None, ("parts", "slab"), None, None),
            P(None, ("parts", "slab"), None, None),
            P(None, ("parts", "slab"), None, None),
            P(("parts", "slab"), None, None),
            P(),
            P(),
            P(),
            P(None, ("parts", "slab")),
            P(("parts", "slab")),
            P(("parts", "slab")),
        ),
        out_specs=(
            P(None, ("parts", "slab"), None, None),
            P(None, ("parts", "slab"), None, None),
            P(("parts", "slab"), None),
        ),
        check_vma=False,
    )
```

profile of v0, /device:TPU:0, one launch (start us, length us, event | category | flops | bytes accessed | tf_op | source)
XLA Modules:
  0.0 695.5 jit_solution(11887543472089410079)
XLA Ops:
  4.8 77.2 %while.15 = (s32[]{:T(128)}, f32[16,8192]{1,0:T(8,128)S(1)}, f32[16,8192]{1,0:T(8,128)}, f32[16,8192]{1,0:T(8,128)}, s32[16,8192]{1,0:T(8,128)S(1)}, /*index=5*/f32[3,77]{1,0:T(4,128)S(1)}, s32[]{:T(128)}, s32[]{:T(128)}) while((s32[]{:T(128)}, f32[16,8192]{1,0:T(8,128)S(1)}, f32[16,8192]{1,0:T(8,128)}, f32[16,8192]{1,0:T(8,128)}, ...), condition=%wide.region_1.2_spmd.clone, body=%wide.region_0.1_spmd.clone.sunk | while | flops 23339088 | bytes 591465 | solution.py:98
  6.1 1.8 dynamic_update_slice.17
  11.0 1.8 dynamic_update_slice.17
  15.8 1.8 dynamic_update_slice.17
  20.6 1.8 dynamic_update_slice.17
  25.4 1.8 dynamic_update_slice.17
  30.3 1.8 dynamic_update_slice.17
  35.1 1.8 dynamic_update_slice.17
  39.9 1.8 dynamic_update_slice.17
  44.8 1.8 dynamic_update_slice.17
  49.6 1.8 dynamic_update_slice.17
  54.4 1.8 dynamic_update_slice.17
  59.2 1.8 dynamic_update_slice.17
  64.1 1.8 dynamic_update_slice.17
  82.1 2.0 multiply_bitcast_fusion
  86.7 3.0 collective-permute-start.1
  93.3 3.8 collective-permute-done.2
  97.8 5.5 collective-permute-start.3
  108.9 6.0 collective-permute-start.5
  120.6 6.5 collective-permute-start.7
  134.4 6.3 collective-permute-start.9
  143.2 3.5 multiply_add_fusion
  155.4 4.3 collective-permute-start.11
  164.9 2.6 add_reduce_fusion
  167.8 4.1 collective-permute-start.12
  173.8 3.3 collective-permute-done.13
  177.1 2.6 fusion.25
  179.7 23.5 %fusion.24 = f32[2,36,64,128]{3,2,1,0:T(8,128)S(1)} fusion(f32[2,36,64,128]{3,2,1,0:T(8,128)} %fusion.25), kind=kLoop, calls=%fused_computation.47 | loop fusion | flops 11796480 | bytes 4718592 | tf_op jit(solution)/shard_map/add | solution.py:159
  203.2 2.5 slice_add_fusion
  205.7 453.2 %gather_fusion = f32[81920]{0:T(1024)S(1)} fusion(f32[131072]{0:T(1024)S(1)} %bitcast.227, s32[81920]{0:T(1024)S(1)} %broadcast_clamp_fusion), kind=kCustom, calls=%fused_computation | custom fusion | bytes 983040 | tf_op jit(solution)/shard_map/jit(_take)/gather | solution.py:175
  661.2 19.1 %all-to-all-start = ((f32[16,10,512]{2,1,0:T(8,128)}), f32[16,10,512]{2,1,0:T(8,128)S(1)}, u32[]{:S(2)}, u32[]{:S(2)}) async-start(f32[16,10,512]{2,1,0:T(8,128)} %fusion.111), calls=%async_computation | async-start | bytes 1048576 | tf_op jit(solution)/shard_map/all_to_all | solution.py:191
  681.6 13.2 %all-to-all-done = f32[16,10,512]{2,1,0:T(8,128)S(1)} async-done(((f32[16,10,512]{2,1,0:T(8,128)}), f32[16,10,512]{2,1,0:T(8,128)S(1)}, u32[]{:S(2)}, u32[]{:S(2)}) %all-to-all-start) | async-done | bytes 327712 | tf_op jit(solution)/shard_map/all_to_all | solution.py:191
  (333 shorter events, 104.5 us)
Async XLA Ops:
  1.5 3.3 copy-start.46
  1.5 3.3 copy-start.47
  1.5 83.5 %collective-permute-start = (f32[2,1,64,128]{3,2,1,0:T(8,128)S(1)}, f32[2,1,64,128]{3,2,1,0:T(8,128)S(1)}, u32[]{:S(2)}, u32[]{:S(2)}) collective-permute-start(f32[2,1,64,128]{3,2,1,0:T(8,128)S(1)} %slice.520), channel_id=1, source_target_pairs={{1,0},{2,1},{3,2},{4,3},{5,4},{6,5},{7,6},{8,7},{9,8},{10,9},{11,1... | collective-permute-start | bytes 196616 | tf_op jit(solution)/shard_map/ppermute | solution.py:22
  86.7 3.9 collective-permute-start.1
  90.2 14.0 %copy-start.15 = (f32[16,64,128]{2,1,0:T(8,128)}, f32[16,64,128]{2,1,0:T(8,128)S(1)}, u32[]{:S(2)}) copy-start(f32[16,64,128]{2,1,0:T(8,128)S(1)} %get-tuple-element.73) | copy-start | bytes 1572868
  91.3 12.8 %copy-start.10 = (f32[16,64,128]{2,1,0:T(8,128)}, f32[16,64,128]{2,1,0:T(8,128)S(1)}, u32[]{:S(2)}) copy-start(f32[16,64,128]{2,1,0:T(8,128)S(1)} %get-tuple-element.79) | copy-start | bytes 1572868
  91.3 12.8 %copy-start.12 = (f32[16,64,128]{2,1,0:T(8,128)}, f32[16,64,128]{2,1,0:T(8,128)S(1)}, u32[]{:S(2)}) copy-start(f32[16,64,128]{2,1,0:T(8,128)S(1)} %get-tuple-element.80) | copy-start | bytes 1572868
  91.3 5.7 collective-permute-start.2
  97.8 6.4 collective-permute-start.3
  105.0 10.8 %copy-start.17 = (f32[16,64,128]{2,1,0:T(8,128)}, f32[16,64,128]{2,1,0:T(8,128)S(1)}, u32[]{:S(2)}) copy-start(f32[16,64,128]{2,1,0:T(8,128)S(1)} %get-tuple-element.96) | copy-start | bytes 1572868
  105.0 3.1 collective-permute-start.4
  108.9 6.9 collective-permute-start.5
  116.6 11.2 %copy-start.19 = (f32[16,64,128]{2,1,0:T(8,128)}, f32[16,64,128]{2,1,0:T(8,128)S(1)}, u32[]{:S(2)}) copy-start(f32[16,64,128]{2,1,0:T(8,128)S(1)} %get-tuple-element.93) | copy-start | bytes 1572868
  116.7 3.1 collective-permute-start.6
  119.8 7.3 %copy-start.45 = (s32[3,160]{1,0:T(4,128)S(1)}, s32[3,160]{1,0:T(4,128)}, u32[]{:S(2)}) copy-start(s32[3,160]{1,0:T(4,128)} %param.21) | copy-start | bytes 5764
  120.6 7.2 %collective-permute-start.7 = (f32[2,1,64,128]{3,2,1,0:T(8,128)S(1)}, f32[2,1,64,128]{3,2,1,0:T(8,128)S(1)}, u32[]{:S(2)}, u32[]{:S(2)}) collective-permute-start(f32[2,1,64,128]{3,2,1,0:T(8,128)S(1)} %pad_maximum_fusion.12), channel_id=1, source_target_pairs={{0,1},{1,2},{2,3},{3,4},{4,5},{5,6},{6,7},{7,8},{8,9},{9,10},{10,1... | collective-permute-start | bytes 196616 | tf_op jit(solution)/shard_map/ppermute | solution.py:22
  128.7 3.1 collective-permute-start.8
  134.4 8.8 %collective-permute-start.9 = (f32[2,1,64,128]{3,2,1,0:T(8,128)S(1)}, f32[2,1,64,128]{3,2,1,0:T(8,128)S(1)}, u32[]{:S(2)}, u32[]{:S(2)}) collective-permute-start(f32[2,1,64,128]{3,2,1,0:T(8,128)S(1)} %pad_maximum_fusion.10), channel_id=1, source_target_pairs={{0,1},{1,2},{2,3},{3,4},{4,5},{5,6},{6,7},{7,8},{8,9},{9,10},{10,1... | collective-permute-start | bytes 196616 | tf_op jit(solution)/shard_map/ppermute | solution.py:22
  148.1 5.5 collective-permute-start.10
  155.4 6.4 copy-start.25
  155.4 6.4 copy-start.27
  155.4 6.4 copy-start.34
  155.4 5.3 copy-start.37
  155.4 5.4 copy-start.43
  155.4 6.3 collective-permute-start.11
  167.6 5.8 copy-start.44
  167.8 6.0 collective-permute-start.12
  171.9 5.2 collective-permute-start.13
  659.1 21.2 %copy-start.26 = (f32[16,64,128]{2,1,0:T(8,128)S(1)}, f32[16,64,128]{2,1,0:T(8,128)}, u32[]{:S(2)}) copy-start(f32[16,64,128]{2,1,0:T(8,128)} %copy-done.25) | copy-start | bytes 1572868
  659.1 21.2 %copy-start.28 = (f32[16,64,128]{2,1,0:T(8,128)S(1)}, f32[16,64,128]{2,1,0:T(8,128)}, u32[]{:S(2)}) copy-start(f32[16,64,128]{2,1,0:T(8,128)} %copy-done.27) | copy-start | bytes 1572868
  659.1 21.2 %copy-start.35 = (f32[16,64,128]{2,1,0:T(8,128)S(1)}, f32[16,64,128]{2,1,0:T(8,128)}, u32[]{:S(2)}) copy-start(f32[16,64,128]{2,1,0:T(8,128)} %copy-done.34) | copy-start | bytes 1572868
  661.2 33.6 %all-to-all-start = ((f32[16,10,512]{2,1,0:T(8,128)}), f32[16,10,512]{2,1,0:T(8,128)S(1)}, u32[]{:S(2)}, u32[]{:S(2)}) async-start(f32[16,10,512]{2,1,0:T(8,128)} %fusion.111), calls=%async_computation | async-start | bytes 1048576 | tf_op jit(solution)/shard_map/all_to_all | solution.py:191
  (32 other events, 60.1 us)
where the time goes:
time: 698 us; the launch traced here: 696 us
  local copies, waits for them, and re-layouts  533 us (76%)
  starting transfers between devices  64.2 us (9%)
  other arithmetic  48.4 us (7%)
  waiting for transfers between devices  26.5 us (4%)
  matrix products  20.2 us (3%)
    gather x3, local copies, waits for them, and re-layouts, body(): jnp.take(sar_avg.reshape(-1), flat_index.reshape(count_slots, edge ** 3),...  453 us
    dynamic_update_slice x48, local copies, waits for them, and re-layouts, materials(): sigma_rows, eps_rows, mass_rows = lax.map(one_layer, layers)  58.9 us
    ppermute x12, starting transfers between devices, shifted(): return lax.ppermute(block, axis, route)  39.5 us
    add x1, other arithmetic, body(): along_y = along_y + padded_y[:, :, offset:offset + across_y]  23.5 us
    all_to_all x1, starting transfers between devices, body(): lax.all_to_all(outgoing, 'slab', split_axis=0, concat_axis=0, tiled=True)  19.1 us
    dot_general x16, matrix products, one_layer(): product = jnp.dot(table, onehot, precision=lax.Precision.HIGHEST)  16.4 us
  transfers between devices with their start and end apart: 15, of which 10 were waited for; matrix products, arithmetic and copies ran while one was open for 13% of the time, Pallas kernels for 0%

commit v1 on v0

v1 whole, which is shorter than its diff:
```python
import functools
import math

import jax
import jax.numpy as jnp
import numpy as np
from jax import lax
from jax.experimental import pallas as pl
from jax.experimental.pallas import tpu as pltpu
from jax.sharding import PartitionSpec as P

STEPS = 6
APRON = 10
BRICK = 8
PERIOD = 2600
START = 325
COURANT = 0.5
FLOOR_SHARE = 0.2
PAD = 8
LANES = 128
F32 = jnp.float32
VMEM_SPEC = pl.BlockSpec(memory_space=pltpu.VMEM)
SMEM_SPEC = pl.BlockSpec(memory_space=pltpu.SMEM)
ANY_SPEC = pl.BlockSpec(memory_space=pl.ANY)
VMEM_LIMIT = 48 * 1024 * 1024


def band(across_z):
    row = lax.broadcasted_iota(jnp.int32, (across_z, across_z), 0)
    col = lax.broadcasted_iota(jnp.int32, (across_z, across_z), 1)
    return (jnp.abs(row - col) <= APRON).astype(F32)


def along_z(rows, matrix):
    return jnp.dot(rows, matrix, precision=lax.Precision.HIGHEST, preferred_element_type=F32)


def clear_margins(padded):
    layers, rows, lanes = padded.shape
    zero = jnp.zeros((layers, 16, lanes), F32)
    padded[:, 0:16] = zero
    padded[:, rows - 16 : rows] = zero


def along_y(padded, triples, layer, across_y):
    count = across_y + 24
    triples[layer, 0:count] = (
        padded[layer, 0:count] + padded[layer, 1 : count + 1] + padded[layer, 2 : count + 2]
    )
    total = triples[layer, 6 : 6 + across_y]
    for part in range(1, 7):
        total = total + triples[layer, 6 + 3 * part : 6 + 3 * part + across_y]
    return total


def window_21(layers, count):
    two = [a + b for a, b in zip(layers[:-1], layers[1:])]
    four = [a + b for a, b in zip(two[:-2], two[2:])]
    eight = [a + b for a, b in zip(four[:-4], four[4:])]
    return [
        (eight[i] + eight[i + 8]) + (four[i + 16] + layers[i + 20]) for i in range(count)
    ]


def material_kernel(tables, tissue, keep, curl, sigma, mass, padded, triples):
    width, across_y, across_z = tissue.shape
    shape = (8, LANES)
    sig = jnp.broadcast_to(tables[0:1, :], shape)
    eps = 1.0 + jnp.broadcast_to(tables[1:2, :], shape)
    rho = jnp.broadcast_to(tables[2:3, :], shape)
    damping = sig / (2.0 * eps)
    keep_row = (1.0 - damping) / (1.0 + damping)
    curl_row = COURANT / (eps * (1.0 + damping))
    clear_margins(padded)
    matrix = band(across_z)

    def one_layer(layer, carry):
        for y in range(0, across_y, 8):
            ids = tissue[layer, y : y + 8, :]
            keep[layer, y : y + 8, :] = jnp.take_along_axis(keep_row, ids, axis=1)
            curl[layer, y : y + 8, :] = jnp.take_along_axis(curl_row, ids, axis=1)
            sigma[layer, y : y + 8, :] = jnp.take_along_axis(sig, ids, axis=1)
            padded[layer, 16 + y : 24 + y, :] = jnp.take_along_axis(rho, ids, axis=1)
        return carry

    lax.fori_loop(0, width, one_layer, 0)

    def sum_z(group, carry):
        layers = pl.ds(group * 4, 4)
        rows = padded[layers, 16 : 16 + across_y, :].reshape(4 * across_y, across_z)
        padded[layers, 16 : 16 + across_y, :] = along_z(rows, matrix).reshape(
            4, across_y, across_z
        )
        return carry

    lax.fori_loop(0, width // 4, sum_z, 0)

    def sum_y(layer, carry):
        mass[layer] = along_y(padded, triples, layer, across_y)
        return carry

    lax.fori_loop(0, width, sum_y, 0)


def field_kernel(
    n,
    phase,
    e_in,
    h_in,
    re_in,
    im_in,
    keep,
    curl,
    sigma,
    mass,
    e_out,
    h_out,
    sar,
    E,
    H,
    re,
    im,
    e_hi,
    e_lo,
    h_lo,
    padded,
    triples,
    heat,
    weight,
    local_sem,
    send_sem,
    hi_sem,
    lo_sem,
    first_sem,
    halo_sem,
):
    width, ny, nz = keep.shape
    last = width - 1
    rows = pl.ds(PAD, ny)
    me = lax.axis_index("slab")
    prev = jnp.maximum(me - 1, 0)
    after = jnp.minimum(me + 1, n - 1)
    has_prev = me > 0
    has_next = me < n - 1

    loads = [
        pltpu.make_async_copy(e_in, E.at[:, :, rows], local_sem.at[0]),
        pltpu.make_async_copy(h_in, H.at[:, :, rows], local_sem.at[1]),
        pltpu.make_async_copy(re_in, re, local_sem.at[2]),
        pltpu.make_async_copy(im_in, im, local_sem.at[3]),
    ]
    for copy in loads:
        copy.start()
    margin = jnp.zeros((3, width, PAD, nz), F32)
    for field in (E, H):
        field[:, :, 0:PAD] = margin
        field[:, :, PAD + ny : 2 * PAD + ny] = margin
    e_hi[...] = jnp.zeros_like(e_hi)
    e_lo[...] = jnp.zeros_like(e_lo)
    h_lo[...] = jnp.zeros_like(h_lo)
    apron = jnp.zeros((APRON, ny, nz), F32)
    for block in (heat, weight):
        block[0:APRON] = apron
        block[APRON + width : 2 * APRON + width] = apron
    clear_margins(padded)

    barrier = pltpu.get_barrier_semaphore()

    @pl.when(has_prev)
    def _():
        pl.semaphore_signal(barrier, inc=1, device_id={"slab": prev})

    @pl.when(has_next)
    def _():
        pl.semaphore_signal(barrier, inc=1, device_id={"slab": after})

    pl.semaphore_wait(barrier, has_prev.astype(jnp.int32) + has_next.astype(jnp.int32))

    def down(slot):
        return pltpu.make_async_remote_copy(
            E.at[pl.ds(1, 2), 0, rows], e_hi.at[slot], send_sem.at[0], hi_sem.at[slot],
            device_id={"slab": prev},
        )

    def up(slot):
        return pltpu.make_async_remote_copy(
            E.at[:, last, rows], e_lo.at[slot, :, pl.ds(0, ny)], send_sem.at[1], lo_sem.at[slot],
            device_id={"slab": after},
        )

    first = pltpu.make_async_remote_copy(
        H.at[pl.ds(1, 2), last, rows], h_lo, first_sem.at[0], first_sem.at[1],
        device_id={"slab": after},
    )

    def halo_down(block, at):
        return pltpu.make_async_remote_copy(
            block.at[pl.ds(APRON, APRON)], block.at[pl.ds(APRON + width, APRON)],
            halo_sem.at[at], halo_sem.at[at + 1], device_id={"slab": prev},
        )

    def halo_up(block, at):
        return pltpu.make_async_remote_copy(
            block.at[pl.ds(width, APRON)], block.at[pl.ds(0, APRON)],
            halo_sem.at[at + 2], halo_sem.at[at + 3], device_id={"slab": after},
        )

    loads[0].wait()
    loads[1].wait()

    @pl.when(has_prev)
    def _():
        down(0).start()

    @pl.when(has_next)
    def _():
        up(0).start()
        first.start()

    weight[APRON : APRON + width] = mass[...]

    @pl.when(has_prev)
    def _():
        halo_down(weight, 4).start()

    @pl.when(has_next)
    def _():
        halo_up(weight, 4).start()

    lane = lax.broadcasted_iota(jnp.int32, (ny, nz), 1)
    not_last = (lane < nz - 1).astype(F32)
    not_first = (lane > 0).astype(F32)

    def z_up(a):
        return pltpu.roll(a, nz - 1, 1) * not_last

    def z_down(a):
        return pltpu.roll(a, 1, 1) * not_first

    def body_of(field, part, layer):
        return field[part, layer, PAD : PAD + ny]

    def y_up(field, part, layer):
        return field[part, layer, PAD + 1 : PAD + 1 + ny]

    def y_down(field, part, layer):
        return field[part, layer, PAD - 1 : PAD - 1 + ny]

    def put(field, part, layer, value):
        field[part, layer, PAD : PAD + ny] = value

    def magnetic(layer, ey_next, ez_next):
        ex, ey, ez = (body_of(E, part, layer) for part in range(3))
        put(H, 0, layer, body_of(H, 0, layer)
            - COURANT * ((y_up(E, 2, layer) - ez) - (z_up(ey) - ey)))
        put(H, 1, layer, body_of(H, 1, layer)
            - COURANT * ((z_up(ex) - ex) - (ez_next - ez)))
        put(H, 2, layer, body_of(H, 2, layer)
            - COURANT * ((ey_next - ey) - (y_up(E, 0, layer) - ex)))

    def magnetic_at(layer):
        magnetic(layer, body_of(E, 1, layer + 1), body_of(E, 2, layer + 1))

    def electric(layer, hy_prev, hz_prev):
        hx, hy, hz = (body_of(H, part, layer) for part in range(3))
        k, c = (keep[layer], curl[layer])
        ex = k * body_of(E, 0, layer) + c * ((hz - y_down(H, 2, layer)) - (hy - z_down(hy)))
        put(E, 0, layer, ex)
        ey = k * body_of(E, 1, layer) + c * ((hx - z_down(hx)) - (hz - hz_prev))
        put(E, 1, layer, ey)
        ez = k * body_of(E, 2, layer) + c * ((hy - hy_prev) - (hx - y_down(H, 0, layer)))
        put(E, 2, layer, ez)

    def electric_at(layer):
        electric(layer, body_of(H, 1, layer - 1), body_of(H, 2, layer - 1))

    def phasor(step, layer):
        for part in range(3):
            value = body_of(E, part, layer)
            re[part, layer] = re[part, layer] + phase[step, 0] * value
            im[part, layer] = im[part, layer] - phase[step, 1] * value

    live = has_prev.astype(F32)

    def one_step(step, carry):
        @pl.when(has_next)
        def _():
            down(step).wait_recv()

        @pl.when(has_prev)
        def _():
            up(step).wait_recv()

        @pl.when(has_prev & (step == 0))
        def _():
            first.wait_recv()

        ex = e_lo[step, 0, 0:ny]
        h_lo[0] = live * (
            h_lo[0]
            - COURANT * ((z_up(ex) - ex) - (body_of(E, 2, 0) - e_lo[step, 2, 0:ny]))
        )
        h_lo[1] = live * (
            h_lo[1]
            - COURANT
            * ((body_of(E, 1, 0) - e_lo[step, 1, 0:ny]) - (e_lo[step, 0, 1 : ny + 1] - ex))
        )
        @pl.when(has_next & (step == 0))
        def _():
            first.wait_send()

        magnetic_at(0)
        magnetic_at(last - 1)
        magnetic(last, e_hi[step, 0], e_hi[step, 1])

        @pl.when(has_prev)
        def _():
            down(step).wait_send()

        @pl.when(has_next)
        def _():
            up(step).wait_send()

        electric(0, h_lo[0], h_lo[1])
        electric_at(last)

        @pl.when(has_prev & (step < STEPS - 1))
        def _():
            down(step + 1).start()

        @pl.when(has_next & (step < STEPS - 1))
        def _():
            up(step + 1).start()

        @pl.when(step == 0)
        def _():
            loads[2].wait()
            loads[3].wait()

        def inner(layer, carry):
            magnetic_at(layer)
            electric_at(layer)
            phasor(step, layer)
            return carry

        lax.fori_loop(1, last - 1, inner, 0)
        electric_at(last - 1)
        phasor(step, last - 1)
        phasor(step, 0)
        phasor(step, last)
        return carry

    lax.fori_loop(0, STEPS, one_step, 0)

    stores = [
        pltpu.make_async_copy(E.at[:, :, rows], e_out, local_sem.at[0]),
        pltpu.make_async_copy(H.at[:, :, rows], h_out, local_sem.at[1]),
    ]
    for copy in stores:
        copy.start()

    matrix = band(nz)

    def heat_z(group, carry):
        layers = pl.ds(group * 4, 4)
        total = jnp.zeros((4, ny, nz), F32)
        for part in range(3):
            real, imag = (re[part, layers], im[part, layers])
            total = total + (real * real + imag * imag)
        total = (0.5 * sigma[layers]) * total
        padded[layers, 16 : 16 + ny, :] = along_z(total.reshape(4 * ny, nz), matrix).reshape(
            4, ny, nz
        )
        return carry

    lax.fori_loop(0, width // 4, heat_z, 0)

    def heat_y(layer, carry):
        heat[APRON + layer] = along_y(padded, triples, layer, ny)
        return carry

    lax.fori_loop(0, width, heat_y, 0)

    @pl.when(has_prev)
    def _():
        halo_down(heat, 0).start()
        halo_down(weight, 4).wait_send()

    @pl.when(has_next)
    def _():
        halo_up(heat, 0).start()
        halo_up(weight, 4).wait_send()
        halo_down(weight, 4).wait_recv()

    @pl.when(has_prev)
    def _():
        halo_up(weight, 4).wait_recv()

    floor_mass = FLOOR_SHARE * (2 * APRON + 1) ** 3

    def weigh(block, carry):
        at = pl.ds(pl.multiple_of(block * 8, 8), 8)
        sums = window_21([weight[i, at] for i in range(width + 2 * APRON)], width)
        for i in range(width):
            sar[i, at] = 1.0 / jnp.maximum(sums[i], floor_mass)
        return carry

    lax.fori_loop(0, ny // 8, weigh, 0)

    @pl.when(has_prev)
    def _():
        halo_down(heat, 0).wait_send()
        halo_up(heat, 0).wait_recv()

    @pl.when(has_next)
    def _():
        halo_up(heat, 0).wait_send()
        halo_down(heat, 0).wait_recv()

    def average(block, carry):
        at = pl.ds(pl.multiple_of(block * 8, 8), 8)
        sums = window_21([heat[i, at] for i in range(width + 2 * APRON)], width)
        for i in range(width):
            sar[i, at] = sums[i] * sar[i, at]
        return carry

    lax.fori_loop(0, ny // 8, average, 0)
    for copy in stores:
        copy.wait()


def brick_kernel(n, codes, sar, table, outgoing, landed, send_sem, recv_sem):
    capacity = outgoing.shape[1]
    me = lax.axis_index("slab")
    barrier = pltpu.get_barrier_semaphore()

    def greet(k, carry):
        pl.semaphore_signal(barrier, inc=1, device_id={"slab": lax.rem(me + k, n)})
        return carry

    lax.fori_loop(1, n, greet, 0)

    shape = (8, LANES)
    lane = lax.broadcasted_iota(jnp.int32, shape, 1)
    sub = lax.broadcasted_iota(jnp.int32, shape, 0)
    even = ((lane - 8 * sub) >= 0) & ((lane - 8 * sub) < 8)
    odd = ((lane - 8 * sub) >= 64) & ((lane - 8 * sub) < 72)

    def one_row(helper, rank):
        code = codes[helper * capacity + rank]
        z = lax.bitwise_and(lax.shift_right_logical(code, 1), 127)
        y = lax.bitwise_and(lax.shift_right_logical(code, 8), 63)
        x = lax.shift_right_logical(code, 14)
        listed = lax.bitwise_and(code, 1).astype(F32)
        from_even = lax.bitwise_and(lane - 8 * sub + z, LANES - 1)
        from_odd = lax.bitwise_and(lane - 8 * sub + (z + 64), LANES - 1)
        for pair in range(BRICK // 2):
            first = jnp.take_along_axis(sar[x + 2 * pair, pl.ds(y, 8), :], from_even, axis=1)
            second = jnp.take_along_axis(sar[x + 2 * pair + 1, pl.ds(y, 8), :], from_odd, axis=1)
            both = jnp.where(even, first, jnp.where(odd, second, 0.0))
            outgoing[helper, pl.ds(rank, 1), pair * LANES : (pair + 1) * LANES] = listed * jnp.sum(
                both, axis=0, keepdims=True
            )

    def fill(helper):
        for rank in range(capacity):
            one_row(helper, rank)

    def copy_to(k):
        helper = lax.rem(me + k, n)
        return pltpu.make_async_remote_copy(
            outgoing.at[helper], landed.at[me], send_sem.at[k], recv_sem.at[me],
            device_id={"slab": helper},
        )

    fill(lax.rem(me + 1, n))
    pl.semaphore_wait(barrier, n - 1)
    copy_to(1).start()

    def send(k, carry):
        fill(lax.rem(me + k, n))
        copy_to(k).start()
        return carry

    lax.fori_loop(2, n, send, 0)
    fill(me)
    landed[me] = outgoing[me]

    def finish(k, carry):
        copy_to(k).wait_send()
        source = lax.rem(me + k, n)
        pltpu.make_async_remote_copy(
            outgoing.at[source], landed.at[source], send_sem.at[k], recv_sem.at[source],
            device_id={"slab": source},
        ).wait_recv()
        return carry

    lax.fori_loop(1, n, finish, 0)
    for source in range(n):
        table[source * capacity : (source + 1) * capacity, :] = landed[source]


def body(
    e_field,
    h_field,
    phasor_re,
    phasor_im,
    tissue,
    sigma_table,
    eps_table,
    density_table,
    brick_anchor,
    brick_helper,
    brick_count,
):
    width, ny, nz = tissue.shape
    n = lax.axis_size("slab")
    grid = jax.ShapeDtypeStruct((width, ny, nz), F32)
    fields = jax.ShapeDtypeStruct(e_field.shape, F32)
    ends = (1, LANES - 1 - sigma_table.shape[0])
    tables = jnp.stack(
        [jnp.pad(sigma_table, ends), jnp.pad(eps_table - 1.0, ends), jnp.pad(density_table, ends)]
    )
    padded = pltpu.VMEM((width, ny + 32, nz), F32)
    params = functools.partial(pltpu.CompilerParams, vmem_limit_bytes=VMEM_LIMIT)

    count_slots = brick_helper.shape[0]
    capacity = max(2, (count_slots + n - 1) // n)
    slot = jnp.arange(count_slots, dtype=jnp.int32)
    earlier = (brick_helper[:, None] == brick_helper[None, :]) & (slot[None, :] < slot[:, None])
    rank = jnp.sum(earlier.astype(jnp.int32), axis=1)
    target = jnp.where(slot < brick_count[0], brick_helper * capacity + rank, -1)
    code = (brick_anchor[0] * 64 + brick_anchor[1]) * 256 + brick_anchor[2] * 2 + 1
    table_rows = jnp.arange(n * capacity, dtype=jnp.int32)
    codes = jnp.sum(jnp.where(table_rows[:, None] == target[None, :], code[None, :], 0), axis=1)

    keep, curl, sigma, mass = pl.pallas_call(
        material_kernel,
        out_shape=[grid] * 4,
        in_specs=[VMEM_SPEC] * 2,
        out_specs=[VMEM_SPEC] * 4,
        scratch_shapes=[padded, padded],
        compiler_params=params(),
        name="materials",
    )(tables, tissue)

    angles = [2.0 * math.pi * (START + step + 1) / PERIOD for step in range(STEPS)]
    phase = jnp.asarray(np.array([[math.cos(t), math.sin(t)] for t in angles], np.float32))
    wide = pltpu.VMEM((width + 2 * APRON, ny, nz), F32)
    electric, magnetic, sar = pl.pallas_call(
        functools.partial(field_kernel, n),
        out_shape=[fields, fields, grid],
        in_specs=[SMEM_SPEC] + [ANY_SPEC] * 4 + [VMEM_SPEC] * 4,
        out_specs=[ANY_SPEC, ANY_SPEC, VMEM_SPEC],
        scratch_shapes=[
            pltpu.VMEM((3, width, ny + 2 * PAD, nz), F32),
            pltpu.VMEM((3, width, ny + 2 * PAD, nz), F32),
            pltpu.VMEM((3, width, ny, nz), F32),
            pltpu.VMEM((3, width, ny, nz), F32),
            pltpu.VMEM((STEPS, 2, ny, nz), F32),
            pltpu.VMEM((STEPS, 3, ny + PAD, nz), F32),
            pltpu.VMEM((2, ny, nz), F32),
            padded,
            padded,
            wide,
            wide,
            pltpu.SemaphoreType.DMA((4,)),
            pltpu.SemaphoreType.DMA((2,)),
            pltpu.SemaphoreType.DMA((STEPS,)),
            pltpu.SemaphoreType.DMA((STEPS,)),
            pltpu.SemaphoreType.DMA((2,)),
            pltpu.SemaphoreType.DMA((8,)),
        ],
        compiler_params=params(collective_id=0, has_side_effects=True),
        name="fields",
    )(phase, e_field, h_field, phasor_re, phasor_im, keep, curl, sigma, mass)

    edge = BRICK**3
    sar_table = pl.pallas_call(
        functools.partial(brick_kernel, n),
        out_shape=jax.ShapeDtypeStruct((n * capacity, edge), F32),
        in_specs=[SMEM_SPEC, VMEM_SPEC],
        out_specs=VMEM_SPEC,
        scratch_shapes=[
            pltpu.VMEM((n, capacity, edge), F32),
            pltpu.VMEM((n, capacity, edge), F32),
            pltpu.SemaphoreType.DMA((n,)),
            pltpu.SemaphoreType.DMA((n,)),
        ],
        compiler_params=params(collective_id=1, has_side_effects=True),
        name="bricks",
    )(codes, sar)
    return (electric, magnetic, sar_table)


def solution(mesh):
    block = P(None, ("parts", "slab"), None, None)
    layers = P(("parts", "slab"), None, None)
    slots = P(("parts", "slab"))
    return jax.shard_map(
        body,
        mesh=mesh,
        in_specs=(
            block,
            block,
            block,
            block,
            layers,
            P(),
            P(),
            P(),
            P(None, ("parts", "slab")),
            slots,
            slots,
        ),
        out_specs=(block, block, P(("parts", "slab"), None)),
        check_vma=False,
    )
```

time: 698 us -> 73.4 us (0.11)
  the two profiles are of different devices: /device:TPU:0 before, /device:TPU:13 now
where the time goes in v1:
time: 73.4 us; the launch traced here: 73.1 us
  Pallas kernels  64.6 us (88%)
  local copies, waits for them, and re-layouts  6.2 us (8%)
  between operations  1.36 us (2%)
  other arithmetic  0.99 us (1%)
    pallas_call x1, Pallas kernels, body(): pl.pallas_call(functools.partial(field_kernel, n), out_shape=[fields, fie...  40.1 us
    pallas_call x1, Pallas kernels, body(): pl.pallas_call(functools.partial(brick_kernel, n), out_shape=jax.ShapeDty...  21.1 us
    unnamed x11, local copies, waits for them, and re-layouts  4.74 us
    pallas_call x1, Pallas kernels, body(): pl.pallas_call(material_kernel, out_shape=[grid] * 4, in_specs=[VMEM_SPEC...  3.4 us

profile of v1, /device:TPU:13, one launch (start us, length us, event | category | flops | bytes accessed | tf_op | source)
XLA Modules:
  0.0 73.1 jit_solution(12263771859594884723)
XLA Ops:
  0.6 0.7 broadcast_add_fusion
  1.3 0.7 pad_bitcast_fusion
  2.0 0.7 pad_bitcast_fusion.2
  2.8 0.0 copy-start
  2.8 1.0 %copy-done = s32[16,64,128]{2,1,0:T(8,128)S(1)} copy-done((s32[16,64,128]{2,1,0:T(8,128)S(1)}, s32[16,64,128]{2,1,0:T(8,128)}, u32[]{:S(2)}) %copy-start) | copy-done | bytes 524312
  3.8 3.4 %materials.1 = (f32[16,64,128]{2,1,0:T(8,128)S(1)}, f32[16,64,128]{2,1,0:T(8,128)S(1)}, f32[16,64,128]{2,1,0:T(8,128)S(1)}, f32[16,64,128]{2,1,0:T(8,128)S(1)}) custom-call(f32[3,128]{1,0:T(4,128)S(1)} %pad_maximum_fusion.tables, s32[16,64,128]{2,1,0:T(8,128)S(1)} %copy-done), custom_call_target="tpu_custom_call" | custom-call | tf_op jit(solution)/shard_map/materials/pallas_call | solution.py:537
  7.2 0.0 copy-start.1
  7.2 0.7 copy-done.1
  7.9 0.0 copy-start.2
  7.9 0.0 copy-start.3
  7.9 40.1 %fields.1 = (f32[3,16,64,128]{3,2,1,0:T(8,128)S(1)}, f32[3,16,64,128]{3,2,1,0:T(8,128)S(1)}, f32[16,64,128]{2,1,0:T(8,128)S(1)}) custom-call(f32[6,2]{1,0:T(8,128)S(1)} %copy-done.1, f32[3,16,64,128]{3,2,1,0:T(8,128)} %e_in.1, f32[3,16,64,128]{3,2,1,0:T(8,128)} %h_in.1, f32[3,16,64,128]{3,2,1,0:T(8,128)} %re_in.1, f32[3,16,64,128]{3,2,1,0:T(8,128)} %im_in.1, ...), custom_call_target="tpu_custom_call" | custom-call | tf_op jit(solution)/shard_map/fields/pallas_call | solution.py:550
  48.0 0.0 copy-done.2
  48.0 0.2 convert_reduce_fusion
  48.9 0.0 copy-done.3
  48.9 0.1 select_reduce_fusion.codes
  49.0 21.1 %bricks.1 = f32[160,512]{1,0:T(8,128)S(1)} custom-call(s32[160]{0:T(256)S(1)} %select_reduce_fusion.codes, f32[16,64,128]{2,1,0:T(8,128)S(1)} %get-tuple-element.16.sar), custom_call_target="tpu_custom_call" | custom-call | tf_op jit(solution)/shard_map/bricks/pallas_call | solution.py:579
  70.1 1.1 %copy.19 = f32[3,16,64,128]{3,2,1,0:T(8,128)} copy(f32[3,16,64,128]{3,2,1,0:T(8,128)S(1)} %get-tuple-element.22) | data formatting | bytes 3145728
  71.3 1.1 %copy.20 = f32[3,16,64,128]{3,2,1,0:T(8,128)} copy(f32[3,16,64,128]{3,2,1,0:T(8,128)S(1)} %get-tuple-element.23) | data formatting | bytes 3145728
  72.4 0.7 copy.21
  (3 shorter events, 0.0 us)
Async XLA Ops:
  2.8 1.0 %copy-start = (s32[16,64,128]{2,1,0:T(8,128)S(1)}, s32[16,64,128]{2,1,0:T(8,128)}, u32[]{:S(2)}) copy-start(s32[16,64,128]{2,1,0:T(8,128)} %tissue.1) | copy-start | bytes 1572868
  7.2 0.7 copy-start.1
  7.9 40.1 %copy-start.2 = (s32[160]{0:T(256)S(1)}, s32[160]{0:T(256)}, u32[]{:S(2)}) copy-start(s32[160]{0:T(256)} %param.21) | copy-start | bytes 1924
  7.9 41.0 %copy-start.3 = (s32[3,160]{1,0:T(4,128)S(1)}, s32[3,160]{1,0:T(4,128)}, u32[]{:S(2)}) copy-start(s32[3,160]{1,0:T(4,128)} %param.20) | copy-start | bytes 5764

commit v2 on v1

--- a/solution.py
+++ b/solution.py
@@ -3,7 +3,6 @@
 
 import jax
 import jax.numpy as jnp
-import numpy as np
 from jax import lax
 from jax.experimental import pallas as pl
 from jax.experimental.pallas import tpu as pltpu
@@ -28,11 +27,17 @@
 def band(across_z):
     row = lax.broadcasted_iota(jnp.int32, (across_z, across_z), 0)
     col = lax.broadcasted_iota(jnp.int32, (across_z, across_z), 1)
-    return (jnp.abs(row - col) <= APRON).astype(F32)
+    return (jnp.abs(row - col) <= APRON).astype(F32).astype(jnp.bfloat16)
 
 
 def along_z(rows, matrix):
-    return jnp.dot(rows, matrix, precision=lax.Precision.HIGHEST, preferred_element_type=F32)
+    high = rows.astype(jnp.bfloat16)
+    rest = rows - high.astype(F32)
+    middle = rest.astype(jnp.bfloat16)
+    low = (rest - middle.astype(F32)).astype(jnp.bfloat16)
+    total = jnp.dot(low, matrix, preferred_element_type=F32)
+    total = total + jnp.dot(middle, matrix, preferred_element_type=F32)
+    return total + jnp.dot(high, matrix, preferred_element_type=F32)
 
 
 def clear_margins(padded):
@@ -62,12 +67,20 @@
     ]
 
 
-def material_kernel(tables, tissue, keep, curl, sigma, mass, padded, triples):
+def material_kernel(
+    sigma_ref, eps_ref, density_ref, tissue, keep, curl, sigma, mass, padded, triples, tables
+):
     width, across_y, across_z = tissue.shape
     shape = (8, LANES)
-    sig = jnp.broadcast_to(tables[0:1, :], shape)
-    eps = 1.0 + jnp.broadcast_to(tables[1:2, :], shape)
-    rho = jnp.broadcast_to(tables[2:3, :], shape)
+    count = sigma_ref.shape[1]
+    tables[...] = jnp.zeros_like(tables)
+    tables[0:1, 0:count] = sigma_ref[...]
+    tables[1:2, 0:count] = eps_ref[...] - 1.0
+    tables[2:3, 0:count] = density_ref[...]
+    shifted = pltpu.roll(tables[...], 1, 1)
+    sig = jnp.broadcast_to(shifted[0:1, :], shape)
+    eps = 1.0 + jnp.broadcast_to(shifted[1:2, :], shape)
+    rho = jnp.broadcast_to(shifted[2:3, :], shape)
     damping = sig / (2.0 * eps)
     keep_row = (1.0 - damping) / (1.0 + damping)
     curl_row = COURANT / (eps * (1.0 + damping))
@@ -104,7 +117,6 @@
 
 def field_kernel(
     n,
-    phase,
     e_in,
     h_in,
     re_in,
@@ -193,15 +205,16 @@
         device_id={"slab": after},
     )
 
-    def halo_down(block, at):
+    def halo_down(block, at, start=0, count=APRON):
         return pltpu.make_async_remote_copy(
-            block.at[pl.ds(APRON, APRON)], block.at[pl.ds(APRON + width, APRON)],
+            block.at[pl.ds(APRON + start, count)],
+            block.at[pl.ds(APRON + width + start, count)],
             halo_sem.at[at], halo_sem.at[at + 1], device_id={"slab": prev},
         )
 
-    def halo_up(block, at):
+    def halo_up(block, at, start=0, count=APRON):
         return pltpu.make_async_remote_copy(
-            block.at[pl.ds(width, APRON)], block.at[pl.ds(0, APRON)],
+            block.at[pl.ds(width + start, count)], block.at[pl.ds(start, count)],
             halo_sem.at[at + 2], halo_sem.at[at + 3], device_id={"slab": after},
         )
 
@@ -218,14 +231,6 @@
         first.start()
 
     weight[APRON : APRON + width] = mass[...]
-
-    @pl.when(has_prev)
-    def _():
-        halo_down(weight, 4).start()
-
-    @pl.when(has_next)
-    def _():
-        halo_up(weight, 4).start()
 
     lane = lax.broadcasted_iota(jnp.int32, (ny, nz), 1)
     not_last = (lane < nz - 1).astype(F32)
@@ -274,11 +279,19 @@
     def electric_at(layer):
         electric(layer, body_of(H, 1, layer - 1), body_of(H, 2, layer - 1))
 
-    def phasor(step, layer):
+    def by_step(step, values):
+        value = jnp.float32(values[0])
+        for at in range(1, STEPS):
+            value = jnp.where(step == at, jnp.float32(values[at]), value)
+        return value
+
+    angles = [2.0 * math.pi * (START + at + 1) / PERIOD for at in range(STEPS)]
+
+    def phasor(step, layer, real, imag):
         for part in range(3):
             value = body_of(E, part, layer)
-            re[part, layer] = re[part, layer] + phase[step, 0] * value
-            im[part, layer] = im[part, layer] - phase[step, 1] * value
+            re[part, layer] = re[part, layer] + real * value
+            im[part, layer] = im[part, layer] - imag * value
 
     live = has_prev.astype(F32)
 
@@ -295,6 +308,8 @@
         def _():
             first.wait_recv()
 
+        real = by_step(step, [math.cos(t) for t in angles])
+        imag = by_step(step, [math.sin(t) for t in angles])
         ex = e_lo[step, 0, 0:ny]
         h_lo[0] = live * (
             h_lo[0]
@@ -327,10 +342,12 @@
         @pl.when(has_prev & (step < STEPS - 1))
         def _():
             down(step + 1).start()
+            halo_down(weight, 4, 2 * step, 2).start()
 
         @pl.when(has_next & (step < STEPS - 1))
         def _():
             up(step + 1).start()
+            halo_up(weight, 4, 2 * step, 2).start()
 
         @pl.when(step == 0)
         def _():
@@ -340,14 +357,14 @@
         def inner(layer, carry):
             magnetic_at(layer)
             electric_at(layer)
-            phasor(step, layer)
+            phasor(step, layer, real, imag)
             return carry
 
         lax.fori_loop(1, last - 1, inner, 0)
         electric_at(last - 1)
-        phasor(step, last - 1)
-        phasor(step, 0)
-        phasor(step, last)
+        phasor(step, last - 1, real, imag)
+        phasor(step, 0, real, imag)
+        phasor(step, last, real, imag)
         return carry
 
     lax.fori_loop(0, STEPS, one_step, 0)
@@ -361,8 +378,8 @@
 
     matrix = band(nz)
 
-    def heat_z(group, carry):
-        layers = pl.ds(group * 4, 4)
+    def heat_group(base):
+        layers = pl.ds(base, 4)
         total = jnp.zeros((4, ny, nz), F32)
         for part in range(3):
             real, imag = (re[part, layers], im[part, layers])
@@ -371,24 +388,33 @@
         padded[layers, 16 : 16 + ny, :] = along_z(total.reshape(4 * ny, nz), matrix).reshape(
             4, ny, nz
         )
-        return carry
-
-    lax.fori_loop(0, width // 4, heat_z, 0)
-
-    def heat_y(layer, carry):
-        heat[APRON + layer] = along_y(padded, triples, layer, ny)
-        return carry
-
-    lax.fori_loop(0, width, heat_y, 0)
+        for layer in range(4):
+            heat[APRON + base + layer] = along_y(padded, triples, base + layer, ny)
+
+    def send_down(start, end):
+        @pl.when(has_prev)
+        def _():
+            halo_down(heat, 0, start, end - start).start()
+
+    def send_up(start, end):
+        @pl.when(has_next)
+        def _():
+            halo_up(heat, 0, start, end - start).start()
+
+    groups = width // 4
+    for base in [0, width - 4] + [4 * i for i in range(1, groups - 1)]:
+        heat_group(base)
+        if base < APRON:
+            send_down(base, min(base + 4, APRON))
+        if base + 4 > width - APRON:
+            send_up(max(base - (width - APRON), 0), base + 4 - (width - APRON))
 
     @pl.when(has_prev)
     def _():
-        halo_down(heat, 0).start()
         halo_down(weight, 4).wait_send()
 
     @pl.when(has_next)
     def _():
-        halo_up(heat, 0).start()
         halo_up(weight, 4).wait_send()
         halo_down(weight, 4).wait_recv()
 
@@ -430,7 +456,7 @@
 
 
 def brick_kernel(n, codes, sar, table, outgoing, landed, send_sem, recv_sem):
-    capacity = outgoing.shape[1]
+    capacity = outgoing.shape[1] // 4
     me = lax.axis_index("slab")
     barrier = pltpu.get_barrier_semaphore()
 
@@ -458,7 +484,7 @@
             first = jnp.take_along_axis(sar[x + 2 * pair, pl.ds(y, 8), :], from_even, axis=1)
             second = jnp.take_along_axis(sar[x + 2 * pair + 1, pl.ds(y, 8), :], from_odd, axis=1)
             both = jnp.where(even, first, jnp.where(odd, second, 0.0))
-            outgoing[helper, pl.ds(rank, 1), pair * LANES : (pair + 1) * LANES] = listed * jnp.sum(
+            outgoing[helper, pl.ds(4 * rank + pair, 1), :] = listed * jnp.sum(
                 both, axis=0, keepdims=True
             )
 
@@ -497,7 +523,11 @@
 
     lax.fori_loop(1, n, finish, 0)
     for source in range(n):
-        table[source * capacity : (source + 1) * capacity, :] = landed[source]
+        at = slice(source * capacity, (source + 1) * capacity)
+        for pair in range(BRICK // 2):
+            table[at, pair * LANES : (pair + 1) * LANES] = landed[
+                source, pl.ds(pair, capacity, stride=4), :
+            ]
 
 
 def body(
@@ -517,10 +547,6 @@
     n = lax.axis_size("slab")
     grid = jax.ShapeDtypeStruct((width, ny, nz), F32)
     fields = jax.ShapeDtypeStruct(e_field.shape, F32)
-    ends = (1, LANES - 1 - sigma_table.shape[0])
-    tables = jnp.stack(
-        [jnp.pad(sigma_table, ends), jnp.pad(eps_table - 1.0, ends), jnp.pad(density_table, ends)]
-    )
     padded = pltpu.VMEM((width, ny + 32, nz), F32)
     params = functools.partial(pltpu.CompilerParams, vmem_limit_bytes=VMEM_LIMIT)
 
@@ -537,20 +563,18 @@
     keep, curl, sigma, mass = pl.pallas_call(
         material_kernel,
         out_shape=[grid] * 4,
-        in_specs=[VMEM_SPEC] * 2,
+        in_specs=[VMEM_SPEC] * 4,
         out_specs=[VMEM_SPEC] * 4,
-        scratch_shapes=[padded, padded],
+        scratch_shapes=[padded, padded, pltpu.VMEM((8, LANES), F32)],
         compiler_params=params(),
         name="materials",
-    )(tables, tissue)
-
-    angles = [2.0 * math.pi * (START + step + 1) / PERIOD for step in range(STEPS)]
-    phase = jnp.asarray(np.array([[math.cos(t), math.sin(t)] for t in angles], np.float32))
+    )(sigma_table[None, :], eps_table[None, :], density_table[None, :], tissue)
+
     wide = pltpu.VMEM((width + 2 * APRON, ny, nz), F32)
     electric, magnetic, sar = pl.pallas_call(
         functools.partial(field_kernel, n),
         out_shape=[fields, fields, grid],
-        in_specs=[SMEM_SPEC] + [ANY_SPEC] * 4 + [VMEM_SPEC] * 4,
+        in_specs=[ANY_SPEC] * 4 + [VMEM_SPEC] * 4,
         out_specs=[ANY_SPEC, ANY_SPEC, VMEM_SPEC],
         scratch_shapes=[
             pltpu.VMEM((3, width, ny + 2 * PAD, nz), F32),
@@ -573,7 +597,7 @@
         ],
         compiler_params=params(collective_id=0, has_side_effects=True),
         name="fields",
-    )(phase, e_field, h_field, phasor_re, phasor_im, keep, curl, sigma, mass)
+    )(e_field, h_field, phasor_re, phasor_im, keep, curl, sigma, mass)
 
     edge = BRICK**3
     sar_table = pl.pallas_call(
@@ -582,8 +606,8 @@
         in_specs=[SMEM_SPEC, VMEM_SPEC],
         out_specs=VMEM_SPEC,
         scratch_shapes=[
-            pltpu.VMEM((n, capacity, edge), F32),
-            pltpu.VMEM((n, capacity, edge), F32),
+            pltpu.VMEM((n, 4 * capacity, LANES), F32),
+            pltpu.VMEM((n, 4 * capacity, LANES), F32),
             pltpu.SemaphoreType.DMA((n,)),
             pltpu.SemaphoreType.DMA((n,)),
         ],

time: 73.4 us -> 63.2 us (0.86)
  the two profiles are of different devices: /device:TPU:13 before, /device:TPU:0 now
where the time goes in v2:
time: 63.2 us; the launch traced here: 62.6 us
  Pallas kernels  54.8 us (87%)
  local copies, waits for them, and re-layouts  6.02 us (10%)
  between operations  1.37 us (2%)
    pallas_call x1, Pallas kernels, body(): pl.pallas_call(functools.partial(field_kernel, n), out_shape=[fields, fie...  30.3 us
    pallas_call x1, Pallas kernels, body(): pl.pallas_call(functools.partial(brick_kernel, n), out_shape=jax.ShapeDty...  21.3 us
    unnamed x15, local copies, waits for them, and re-layouts  6.02 us
    pallas_call x1, Pallas kernels, body(): pl.pallas_call(material_kernel, out_shape=[grid] * 4, in_specs=[VMEM_SPEC...  3.27 us

profile of v2, /device:TPU:0, one launch (start us, length us, event | category | flops | bytes accessed | tf_op | source)
XLA Modules:
  0.0 62.6 jit_solution(16635172051665989703)
XLA Ops:
  0.6 0.0 copy-start
  0.6 1.0 %copy-done = s32[16,64,128]{2,1,0:T(8,128)S(1)} copy-done((s32[16,64,128]{2,1,0:T(8,128)S(1)}, s32[16,64,128]{2,1,0:T(8,128)}, u32[]{:S(2)}) %copy-start) | copy-done | bytes 524312
  1.7 0.0 copy-start.1
  1.7 0.7 %copy-done.1 = f32[77]{0:T(128)S(1)} copy-done((f32[77]{0:T(128)S(1)}, f32[77]{0:T(128)}, u32[]{:S(2)}) %copy-start.1) | copy-done | bytes 332
  2.3 0.0 copy-start.2
  2.3 0.7 %copy-done.2 = f32[77]{0:T(128)S(1)} copy-done((f32[77]{0:T(128)S(1)}, f32[77]{0:T(128)}, u32[]{:S(2)}) %copy-start.2) | copy-done | bytes 332
  3.0 0.0 copy-start.3
  3.0 0.7 %copy-done.3 = f32[77]{0:T(128)S(1)} copy-done((f32[77]{0:T(128)S(1)}, f32[77]{0:T(128)}, u32[]{:S(2)}) %copy-start.3) | copy-done | bytes 332
  3.6 3.3 %materials.1 = (f32[16,64,128]{2,1,0:T(8,128)S(1)}, f32[16,64,128]{2,1,0:T(8,128)S(1)}, f32[16,64,128]{2,1,0:T(8,128)S(1)}, f32[16,64,128]{2,1,0:T(8,128)S(1)}) custom-call(f32[1,77]{1,0:T(1,128)S(1)} %bitcast.6, f32[1,77]{1,0:T(1,128)S(1)} %bitcast.7, f32[1,77]{1,0:T(1,128)S(1)} %bitcast.8, s32[16,64,128]{2,1,0:T(8,128)S(1)} %copy-done), custom_call_target="tpu_custom_call" | custom-call | tf_op jit(solution)/shard_map/materials/pallas_call | solution.py:563
  6.9 0.0 copy-start.4
  6.9 0.0 copy-start.5
  6.9 30.3 %fields.1 = (f32[3,16,64,128]{3,2,1,0:T(8,128)S(1)}, f32[3,16,64,128]{3,2,1,0:T(8,128)S(1)}, f32[16,64,128]{2,1,0:T(8,128)S(1)}) custom-call(f32[3,16,64,128]{3,2,1,0:T(8,128)} %e_in.1, f32[3,16,64,128]{3,2,1,0:T(8,128)} %h_in.1, f32[3,16,64,128]{3,2,1,0:T(8,128)} %re_in.1, f32[3,16,64,128]{3,2,1,0:T(8,128)} %im_in.1, ...), custom_call_target="tpu_custom_call" | custom-call | tf_op jit(solution)/shard_map/fields/pallas_call | solution.py:574
  37.2 0.0 copy-done.4
  37.2 0.2 convert_reduce_fusion
  38.1 0.0 copy-done.5
  38.1 0.1 select_reduce_fusion.codes
  38.2 21.3 %bricks.1 = f32[160,512]{1,0:T(8,128)S(1)} custom-call(s32[160]{0:T(256)S(1)} %select_reduce_fusion.codes, f32[16,64,128]{2,1,0:T(8,128)S(1)} %get-tuple-element.16.sar), custom_call_target="tpu_custom_call" | custom-call | tf_op jit(solution)/shard_map/bricks/pallas_call | solution.py:603
  59.5 1.1 %copy.18 = f32[3,16,64,128]{3,2,1,0:T(8,128)} copy(f32[3,16,64,128]{3,2,1,0:T(8,128)S(1)} %get-tuple-element.20) | data formatting | bytes 3145728
  60.7 1.1 %copy.19 = f32[3,16,64,128]{3,2,1,0:T(8,128)} copy(f32[3,16,64,128]{3,2,1,0:T(8,128)S(1)} %get-tuple-element.21) | data formatting | bytes 3145728
  61.8 0.7 %copy.20 = f32[160,512]{1,0:T(8,128)} copy(f32[160,512]{1,0:T(8,128)S(1)} %bricks.1) | data formatting | bytes 655360
  (2 shorter events, 0.0 us)
Async XLA Ops:
  0.6 1.0 %copy-start = (s32[16,64,128]{2,1,0:T(8,128)S(1)}, s32[16,64,128]{2,1,0:T(8,128)}, u32[]{:S(2)}) copy-start(s32[16,64,128]{2,1,0:T(8,128)} %tissue.1) | copy-start | bytes 1572868
  1.7 0.7 %copy-start.1 = (f32[77]{0:T(128)S(1)}, f32[77]{0:T(128)}, u32[]{:S(2)}) copy-start(f32[77]{0:T(128)} %param.16) | copy-start | bytes 928
  2.3 0.7 %copy-start.2 = (f32[77]{0:T(128)S(1)}, f32[77]{0:T(128)}, u32[]{:S(2)}) copy-start(f32[77]{0:T(128)} %param.17) | copy-start | bytes 928
  3.0 0.7 %copy-start.3 = (f32[77]{0:T(128)S(1)}, f32[77]{0:T(128)}, u32[]{:S(2)}) copy-start(f32[77]{0:T(128)} %param.18) | copy-start | bytes 928
  6.9 30.3 %copy-start.4 = (s32[160]{0:T(256)S(1)}, s32[160]{0:T(256)}, u32[]{:S(2)}) copy-start(s32[160]{0:T(256)} %param.20) | copy-start | bytes 1924
  6.9 31.2 %copy-start.5 = (s32[3,160]{1,0:T(4,128)S(1)}, s32[3,160]{1,0:T(4,128)}, u32[]{:S(2)}) copy-start(s32[3,160]{1,0:T(4,128)} %param.19) | copy-start | bytes 5764

commit v3 on v2

--- a/solution.py
+++ b/solution.py
@@ -67,7 +67,7 @@
     ]
 
 
-def material_kernel(
+def materials(
     sigma_ref, eps_ref, density_ref, tissue, keep, curl, sigma, mass, padded, triples, tables
 ):
     width, across_y, across_z = tissue.shape
@@ -117,17 +117,31 @@
 
 def field_kernel(
     n,
+    codes,
+    sigma_in,
+    eps_in,
+    density_in,
+    tissue_in,
     e_in,
     h_in,
     re_in,
     im_in,
+    e_out,
+    h_out,
+    table,
+    sigma_row,
+    eps_row,
+    density_row,
+    tissue,
+    tables,
     keep,
     curl,
     sigma,
-    mass,
-    e_out,
-    h_out,
     sar,
+    outgoing,
+    landed,
+    row_send,
+    row_recv,
     E,
     H,
     re,
@@ -146,7 +160,7 @@
     first_sem,
     halo_sem,
 ):
-    width, ny, nz = keep.shape
+    width, ny, nz = tissue.shape
     last = width - 1
     rows = pl.ds(PAD, ny)
     me = lax.axis_index("slab")
@@ -160,6 +174,10 @@
         pltpu.make_async_copy(h_in, H.at[:, :, rows], local_sem.at[1]),
         pltpu.make_async_copy(re_in, re, local_sem.at[2]),
         pltpu.make_async_copy(im_in, im, local_sem.at[3]),
+        pltpu.make_async_copy(sigma_in, sigma_row, local_sem.at[4]),
+        pltpu.make_async_copy(eps_in, eps_row, local_sem.at[5]),
+        pltpu.make_async_copy(density_in, density_row, local_sem.at[6]),
+        pltpu.make_async_copy(tissue_in, tissue, local_sem.at[7]),
     ]
     for copy in loads:
         copy.start()
@@ -174,19 +192,15 @@
     for block in (heat, weight):
         block[0:APRON] = apron
         block[APRON + width : 2 * APRON + width] = apron
-    clear_margins(padded)
 
     barrier = pltpu.get_barrier_semaphore()
 
-    @pl.when(has_prev)
-    def _():
-        pl.semaphore_signal(barrier, inc=1, device_id={"slab": prev})
-
-    @pl.when(has_next)
-    def _():
-        pl.semaphore_signal(barrier, inc=1, device_id={"slab": after})
-
-    pl.semaphore_wait(barrier, has_prev.astype(jnp.int32) + has_next.astype(jnp.int32))
+    def greet(k, carry):
+        pl.semaphore_signal(barrier, inc=1, device_id={"slab": lax.rem(me + k, n)})
+        return carry
+
+    lax.fori_loop(1, n, greet, 0)
+    pl.semaphore_wait(barrier, n - 1)
 
     def down(slot):
         return pltpu.make_async_remote_copy(
@@ -230,7 +244,12 @@
         up(0).start()
         first.start()
 
-    weight[APRON : APRON + width] = mass[...]
+    for copy in loads[4:]:
+        copy.wait()
+    materials(
+        sigma_row, eps_row, density_row, tissue, keep, curl, sigma,
+        weight.at[pl.ds(APRON, width)], padded, triples, tables,
+    )
 
     lane = lax.broadcasted_iota(jnp.int32, (ny, nz), 1)
     not_last = (lane < nz - 1).astype(F32)
@@ -451,21 +470,14 @@
         return carry
 
     lax.fori_loop(0, ny // 8, average, 0)
+    send_bricks(n, codes, sar, table, outgoing, landed, row_send, row_recv)
     for copy in stores:
         copy.wait()
 
 
-def brick_kernel(n, codes, sar, table, outgoing, landed, send_sem, recv_sem):
+def send_bricks(n, codes, sar, table, outgoing, landed, send_sem, recv_sem):
     capacity = outgoing.shape[1] // 4
     me = lax.axis_index("slab")
-    barrier = pltpu.get_barrier_semaphore()
-
-    def greet(k, carry):
-        pl.semaphore_signal(barrier, inc=1, device_id={"slab": lax.rem(me + k, n)})
-        return carry
-
-    lax.fori_loop(1, n, greet, 0)
-
     shape = (8, LANES)
     lane = lax.broadcasted_iota(jnp.int32, shape, 1)
     sub = lax.broadcasted_iota(jnp.int32, shape, 0)
@@ -500,7 +512,6 @@
         )
 
     fill(lax.rem(me + 1, n))
-    pl.semaphore_wait(barrier, n - 1)
     copy_to(1).start()
 
     def send(k, carry):
@@ -545,7 +556,6 @@
 ):
     width, ny, nz = tissue.shape
     n = lax.axis_size("slab")
-    grid = jax.ShapeDtypeStruct((width, ny, nz), F32)
     fields = jax.ShapeDtypeStruct(e_field.shape, F32)
     padded = pltpu.VMEM((width, ny + 32, nz), F32)
     params = functools.partial(pltpu.CompilerParams, vmem_limit_bytes=VMEM_LIMIT)
@@ -560,23 +570,29 @@
     table_rows = jnp.arange(n * capacity, dtype=jnp.int32)
     codes = jnp.sum(jnp.where(table_rows[:, None] == target[None, :], code[None, :], 0), axis=1)
 
-    keep, curl, sigma, mass = pl.pallas_call(
-        material_kernel,
-        out_shape=[grid] * 4,
-        in_specs=[VMEM_SPEC] * 4,
-        out_specs=[VMEM_SPEC] * 4,
-        scratch_shapes=[padded, padded, pltpu.VMEM((8, LANES), F32)],
-        compiler_params=params(),
-        name="materials",
-    )(sigma_table[None, :], eps_table[None, :], density_table[None, :], tissue)
-
     wide = pltpu.VMEM((width + 2 * APRON, ny, nz), F32)
-    electric, magnetic, sar = pl.pallas_call(
+    block = pltpu.VMEM((width, ny, nz), F32)
+    entries = pltpu.VMEM((1, sigma_table.shape[0]), F32)
+    rows = pltpu.VMEM((n, 4 * capacity, LANES), F32)
+    return pl.pallas_call(
         functools.partial(field_kernel, n),
-        out_shape=[fields, fields, grid],
-        in_specs=[ANY_SPEC] * 4 + [VMEM_SPEC] * 4,
+        out_shape=[fields, fields, jax.ShapeDtypeStruct((n * capacity, BRICK**3), F32)],
+        in_specs=[SMEM_SPEC] + [ANY_SPEC] * 8,
         out_specs=[ANY_SPEC, ANY_SPEC, VMEM_SPEC],
         scratch_shapes=[
+            entries,
+            entries,
+            entries,
+            pltpu.VMEM((width, ny, nz), jnp.int32),
+            pltpu.VMEM((8, LANES), F32),
+            block,
+            block,
+            block,
+            block,
+            rows,
+            rows,
+            pltpu.SemaphoreType.DMA((n,)),
+            pltpu.SemaphoreType.DMA((n,)),
             pltpu.VMEM((3, width, ny + 2 * PAD, nz), F32),
             pltpu.VMEM((3, width, ny + 2 * PAD, nz), F32),
             pltpu.VMEM((3, width, ny, nz), F32),
@@ -588,7 +604,7 @@
             padded,
             wide,
             wide,
-            pltpu.SemaphoreType.DMA((4,)),
+            pltpu.SemaphoreType.DMA((8,)),
             pltpu.SemaphoreType.DMA((2,)),
             pltpu.SemaphoreType.DMA((STEPS,)),
             pltpu.SemaphoreType.DMA((STEPS,)),
@@ -597,24 +613,17 @@
         ],
         compiler_params=params(collective_id=0, has_side_effects=True),
         name="fields",
-    )(e_field, h_field, phasor_re, phasor_im, keep, curl, sigma, mass)
-
-    edge = BRICK**3
-    sar_table = pl.pallas_call(
-        functools.partial(brick_kernel, n),
-        out_shape=jax.ShapeDtypeStruct((n * capacity, edge), F32),
-        in_specs=[SMEM_SPEC, VMEM_SPEC],
-        out_specs=VMEM_SPEC,
-        scratch_shapes=[
-            pltpu.VMEM((n, 4 * capacity, LANES), F32),
-            pltpu.VMEM((n, 4 * capacity, LANES), F32),
-            pltpu.SemaphoreType.DMA((n,)),
-            pltpu.SemaphoreType.DMA((n,)),
-        ],
-        compiler_params=params(collective_id=1, has_side_effects=True),
-        name="bricks",
-    )(codes, sar)
-    return (electric, magnetic, sar_table)
+    )(
+        codes,
+        sigma_table[None, :],
+        eps_table[None, :],
+        density_table[None, :],
+        tissue,
+        e_field,
+        h_field,
+        phasor_re,
+        phasor_im,
+    )
 
 
 def solution(mesh):

time: 63.2 us -> 62.3 us (0.986)
  Pallas kernels: 54.8 us -> 50.7 us
  other arithmetic: 0.32 us -> 2.55 us
  local copies, waits for them, and re-layouts: 6.02 us -> 7.42 us
    pallas_call x2 -> x0, Pallas kernels: 24.6 us -> none  [the longest x1 21.3 us: body(): pl.pallas_call(functools.partial(brick_kernel, n), out_shape=jax.ShapeDty...]
    pallas_call x1, Pallas kernels: 30.3 us -> 50.7 us  [body(): pl.pallas_call(functools.partial(field_kernel, n), out_shape=[fields, fie...]
    unnamed x15 -> x13, local copies, waits for them, and re-layouts: 6.02 us -> 7.42 us
    add x1, other arithmetic: 0.01 us -> 0.81 us  [body(): (brick_anchor[0] * 64 + brick_anchor[1]) * 256 + brick_anchor[2] * 2 + 1]
    reduce_sum x1, other arithmetic: 0.19 us -> 0.94 us  [body(): rank = jnp.sum(earlier.astype(jnp.int32), axis=1)]
    select_n x1, other arithmetic: 0.01 us -> 0.69 us  [body(): jnp.where(slot < brick_count[0], brick_helper * capacity + rank, -1)]
where the time goes in v3:
time: 62.3 us; the launch traced here: 62 us
  Pallas kernels  50.7 us (81%)
  local copies, waits for them, and re-layouts  7.42 us (12%)
  other arithmetic  2.55 us (4%)
  between operations  1.3 us (2%)
    pallas_call x1, Pallas kernels, body(): pl.pallas_call(functools.partial(field_kernel, n), out_shape=[fields, fie...  50.7 us
    unnamed x13, local copies, waits for them, and re-layouts  7.42 us

profile of v3, /device:TPU:0, one launch (start us, length us, event | category | flops | bytes accessed | tf_op | source)
XLA Modules:
  0.0 62.0 jit_solution(1257818215847224886)
XLA Ops:
  1.3 0.8 %add_add_fusion = s32[1,160]{1,0:T(1,128)S(1)} fusion(s32[3,160]{1,0:T(4,128)} %param.19), kind=kLoop, calls=%fused_computation.6 | loop fusion | flops 960 | bytes 2560 | tf_op jit(solution)/shard_map/add | solution.py:569
  2.1 0.9 %convert_reduce_fusion = s32[160]{0:T(256)S(1)} fusion(s32[160]{0:T(256)} %param.20), kind=kLoop, calls=%fused_computation.1 | loop fusion | flops 127840 | bytes 1280 | tf_op jit(solution)/shard_map/reduce_sum | solution.py:567
  3.0 0.7 %compare_select_fusion = s32[160]{0:T(256)S(1)} fusion(s32[160]{0:T(256)S(1)} %convert_reduce_fusion, s32[160]{0:T(256)} %param.20, s32[]{:T(128)} %bitcast.5), kind=kLoop, calls=%fused_computation.5 | loop fusion | flops 640 | bytes 1924 | tf_op jit(solution)/shard_map/jit(_where)/select_n | solution.py:568
  3.7 0.1 select_reduce_fusion.codes
  3.8 0.0 copy-start
  3.8 1.4 %copy-done = f32[3,16,64,128]{3,2,1,0:T(8,128)S(1)} copy-done((f32[3,16,64,128]{3,2,1,0:T(8,128)S(1)}, f32[3,16,64,128]{3,2,1,0:T(8,128)}, u32[]{:S(2)}) %copy-start) | copy-done | bytes 1572888
  5.2 0.0 copy-start.1
  5.2 1.0 %copy-done.1 = s32[16,64,128]{2,1,0:T(8,128)S(1)} copy-done((s32[16,64,128]{2,1,0:T(8,128)S(1)}, s32[16,64,128]{2,1,0:T(8,128)}, u32[]{:S(2)}) %copy-start.1) | copy-done | bytes 524312
  6.3 0.0 copy-start.2
  6.3 0.7 %copy-done.2 = f32[77]{0:T(128)S(1)} copy-done((f32[77]{0:T(128)S(1)}, f32[77]{0:T(128)}, u32[]{:S(2)}) %copy-start.2) | copy-done | bytes 332
  6.9 0.0 copy-start.3
  6.9 0.7 %copy-done.3 = f32[77]{0:T(128)S(1)} copy-done((f32[77]{0:T(128)S(1)}, f32[77]{0:T(128)}, u32[]{:S(2)}) %copy-start.3) | copy-done | bytes 332
  7.6 0.0 copy-start.4
  7.6 0.7 %copy-done.4 = f32[77]{0:T(128)S(1)} copy-done((f32[77]{0:T(128)S(1)}, f32[77]{0:T(128)}, u32[]{:S(2)}) %copy-start.4) | copy-done | bytes 332
  8.3 50.7 %fields.1 = (f32[3,16,64,128]{3,2,1,0:T(8,128)S(1)}, f32[3,16,64,128]{3,2,1,0:T(8,128)S(1)}, f32[160,512]{1,0:T(8,128)S(1)}) custom-call(s32[160]{0:T(256)S(1)} %select_reduce_fusion.codes, f32[1,77]{1,0:T(1,128)S(1)} %bitcast.6, f32[1,77]{1,0:T(1,128)S(1)} %bitcast.7, f32[1,77]{1,0:T(1,128)S(1)} %bitcast.8, s32[16,64,128]{2,1,0:T(8,128)S(1)} %copy-done.1, ...), custom_call_target="tpu_custom_call" | custom-call | tf_op jit(solution)/shard_map/fields/pallas_call | solution.py:577
  59.0 1.1 %copy.18 = f32[3,16,64,128]{3,2,1,0:T(8,128)} copy(f32[3,16,64,128]{3,2,1,0:T(8,128)S(1)} %get-tuple-element.6) | data formatting | bytes 3145728
  60.1 1.1 %copy.19 = f32[3,16,64,128]{3,2,1,0:T(8,128)} copy(f32[3,16,64,128]{3,2,1,0:T(8,128)S(1)} %get-tuple-element.7) | data formatting | bytes 3145728
  61.3 0.7 %copy.20 = f32[160,512]{1,0:T(8,128)} copy(f32[160,512]{1,0:T(8,128)S(1)} %get-tuple-element.8) | data formatting | bytes 655360
Async XLA Ops:
  3.8 1.4 %copy-start = (f32[3,16,64,128]{3,2,1,0:T(8,128)S(1)}, f32[3,16,64,128]{3,2,1,0:T(8,128)}, u32[]{:S(2)}) copy-start(f32[3,16,64,128]{3,2,1,0:T(8,128)} %e_in.1) | copy-start | bytes 4718596
  5.2 1.0 %copy-start.1 = (s32[16,64,128]{2,1,0:T(8,128)S(1)}, s32[16,64,128]{2,1,0:T(8,128)}, u32[]{:S(2)}) copy-start(s32[16,64,128]{2,1,0:T(8,128)} %tissue_in.1) | copy-start | bytes 1572868
  6.3 0.7 %copy-start.2 = (f32[77]{0:T(128)S(1)}, f32[77]{0:T(128)}, u32[]{:S(2)}) copy-start(f32[77]{0:T(128)} %param.16) | copy-start | bytes 928
  6.9 0.7 %copy-start.3 = (f32[77]{0:T(128)S(1)}, f32[77]{0:T(128)}, u32[]{:S(2)}) copy-start(f32[77]{0:T(128)} %param.17) | copy-start | bytes 928
  7.6 0.7 %copy-start.4 = (f32[77]{0:T(128)S(1)}, f32[77]{0:T(128)}, u32[]{:S(2)}) copy-start(f32[77]{0:T(128)} %param.18) | copy-start | bytes 928
